TPU v7x, 32 devices: a whole 2x2x4 slice. The times are simulated.
32 devices in a mesh: section: 4 (over x, core), shard: 8 (over z, y).
Axes of the slice: x: 2, y: 2, z: 4, core: 2. Of those that a mesh axis runs over, the one named last changes fastest.
Arguments:
- hidden: bfloat16 [256, 8192], P(('section', 'shard')), may hold values from -6 to 6
- norm_gain: float32 [4, 8192], P('section'), may hold values from 0.1 to 1.9
- gate_weight: bfloat16 [4, 8192, 16384], P('section', None, 'shard'), may hold values from -0.0625 to 0.0625
- up_weight: bfloat16 [4, 8192, 16384], P('section', None, 'shard'), may hold values from -0.0625 to 0.0625
- head_vector: bfloat16 [4, 16384], P('section', 'shard'), may hold values from -0.046875 to 0.046875
- pack_slot: int32 [4, 256], replicated, may hold values from 0 to 255, each once within a row
- owner_slot: int32 [256], replicated, may hold values from 0 to 255, each once
Outputs:
- section_scores: float32 [4, 256], P('section', 'shard')
- joined: float32 [4, 256], P(None, ('section', 'shard'))
All inputs are finite; a program needn't handle non-finite values.
Results may differ from a plain program's by a relative error of at most 0.0032.
Values may be sent and summed in bfloat16 or wider, within the bound.
A program may use at most 128 MiB of HBM per device.

v0:
```python
import jax
import jax.numpy as jnp
from jax import lax
from jax.sharding import PartitionSpec as P

epsilon = 1e-06


def normalize(row_block, gain_row):
    widened = row_block.astype(jnp.float32)
    inv_rms = lax.rsqrt(jnp.mean(widened * widened, axis=1, keepdims=True) + epsilon)
    return (widened * inv_rms * gain_row).astype(jnp.bfloat16)


def score_block(normed, gate_cols, up_cols, head_cols):
    gate_out = jnp.dot(normed, gate_cols, preferred_element_type=jnp.float32)
    up_out = jnp.dot(normed, up_cols, preferred_element_type=jnp.float32)
    activated = jax.nn.silu(gate_out) * up_out
    return jnp.dot(activated, head_cols.astype(jnp.float32), precision=lax.Precision.HIGHEST)


def invert(ordering):
    total_rows = ordering.shape[0]
    return (
        jnp.zeros((total_rows,), jnp.int32)
        .at[ordering]
        .set(jnp.arange(total_rows, dtype=jnp.int32))
    )


def body(hidden, norm_gain, gate_weight, up_weight, head_vector, pack_slot, owner_slot):
    gain_row = norm_gain[0]
    gate_cols = gate_weight[0]
    up_cols = up_weight[0]
    head_cols = head_vector[0]
    partial_value = score_block(
        normalize(lax.all_gather(hidden, ("section", "shard"), axis=0, tiled=True), gain_row),
        gate_cols,
        up_cols,
        head_cols,
    )
    section = lax.axis_index("section")
    own_pack = lax.dynamic_index_in_dim(pack_slot, section, 0, keepdims=False)
    inverse = invert(own_pack)
    packed = partial_value[inverse]
    scores = lax.psum_scatter(packed, "shard", scatter_dimension=0, tiled=True)
    flipped = jnp.logical_or(section == 1, section == 3)
    values = jnp.where(flipped, jax.nn.log_sigmoid(scores), scores)
    shards = lax.axis_size("shard")
    sections = lax.axis_size("section")
    pack_rows = values.shape[0]
    total_rows = owner_slot.shape[0]
    own_count = total_rows // (shards * sections)
    first_row = lax.axis_index("shard") * pack_rows
    rows_here = lax.dynamic_slice_in_dim(inverse, first_row, pack_rows)
    targets = owner_slot[rows_here]
    spread = jnp.zeros((total_rows,), jnp.float32).at[targets].set(values)
    spread = spread.reshape(sections * shards, own_count)
    arrived = lax.all_to_all(spread, ("section", "shard"), split_axis=0, concat_axis=0, tiled=True)
    joined = arrived.reshape(sections, shards, own_count).sum(axis=1)
    return (values[None, :], joined)


def solution(mesh):
    in_specs = (
        P(("section", "shard"), None),
        P("section", None),
        P("section", None, "shard"),
        P("section", None, "shard"),
        P("section", "shard"),
        P(),
        P(),
    )
    out_specs = (P("section", "shard"), P(None, ("section", "shard")))
    return jax.shard_map(body, mesh=mesh, in_specs=in_specs, out_specs=out_specs, check_vma=False)
```

profile of v0, /device:TPU:0, one launch (start us, length us, event | category | flops | bytes accessed | tf_op | source)
XLA Modules:
  0.0 152.1 jit_solution(14109968288466194728)
XLA Ops:
  7.2 0.0 copy-start
  7.2 0.0 copy-start.2
  7.2 0.0 all-gather.2.cloned.1.call-start
  7.2 0.7 all-gather.2.cloned.1.call-update
  7.9 1.2 dynamic-slice
  9.8 0.7 compare_select_fusion
  10.5 1.4 scatter_custom_fusion
  11.9 0.1 compare_select_fusion.3
  12.0 1.4 gather_fusion.1
  13.4 62.5 %all-gather.2.cloned.1.call-done = bf16[256,8192]{1,0:T(8,128)(2,1)} async-done(((bf16[8,8192]{1,0:T(8,128)(2,1)}), bf16[256,8192]{1,0:T(8,128)(2,1)}) %all-gather.2.cloned.1.call-update) | async-done | bytes 4194320 | tf_op jit(solution)/shard_map/all_gather | solution.py:37
  75.9 0.0 copy-start.1
  75.9 3.3 %fusion.4 = f32[256]{0:T(256)S(1)} fusion(bf16[256,8192]{1,0:T(8,128)(2,1)} %all-gather.2.cloned.1.call-done), kind=kLoop, calls=%fused_computation.10 | loop fusion | flops 6291200 | bytes 4195328 | tf_op jit(solution)/shard_map/reduce_sum | solution.py:11
  79.2 0.0 copy-done.2
  79.2 0.2 copy-done.1
  79.4 15.6 %fusion.2 = f32[256,2048]{1,0:T(8,128)} fusion(bf16[1,8192,2048]{2,1,0:T(8,128)(2,1)} %param.9, bf16[256,8192]{1,0:T(8,128)(2,1)S(1)} %copy-done.1, f32[8192]{0:T(1024)S(1)} %bitcast.31, f32[256]{0:T(256)S(1)} %add_rsqrt_fusion), kind=kOutput, calls=%fused_computation.6 | convolution fusion | flops 8598323200 | bytes 39879680 | tf_op jit(solution)/shard_map/dot_general | solution.py:16
  94.9 15.7 %fusion.7 = f32[256,2048]{1,0:T(8,128)S(1)} fusion(bf16[1,8192,2048]{2,1,0:T(8,128)(2,1)} %param.10, f32[256,2048]{1,0:T(8,128)} %fusion.2, bf16[256,8192]{1,0:T(8,128)(2,1)S(1)} %copy-done.1, f32[8192]{0:T(1024)S(1)} %bitcast.32, f32[256]{0:T(256)S(1)} %add_rsqrt_fusion), kind=kOutput, calls=%fused_computation.13 | convolution fusion | flops 8600944640 | bytes 41976832 | tf_op jit(solution)/shard_map/dot_general | solution.py:17
  110.6 0.0 copy-done
  110.6 1.0 fusion.12
  111.7 2.0 %gather_fusion = f32[256]{0:T(256)S(1)} fusion(f32[256]{0:T(256)S(1)} %bitcast.28, s32[1024]{0:T(1024)S(1)} %pad_clamp_fusion.1), kind=kCustom, calls=%fused_computation | custom fusion | bytes 3072 | tf_op jit(solution)/shard_map/gather | solution.py:45
  113.6 19.9 %all-reduce = f32[256]{0:T(256)S(1)} all-reduce(f32[256]{0:T(256)S(1)} %gather_fusion), channel_id=2, replica_groups=mesh['section'=4,'shard'=8] {'shard'}, use_global_device_ids=true, to_apply=%region_2.3.clone | all-reduce | flops 256 | bytes 2048
  133.6 0.1 broadcast_select_fusion
  133.6 0.7 scatter_custom_fusion.1
  134.3 0.7 all_to_all.6
  135.0 2.6 %all-to-all-start = ((f32[32,1,8]{2,1,0:T(1,128)}), f32[32,1,8]{2,1,0:T(1,128)S(1)}, u32[]{:S(2)}, u32[]{:S(2)}) async-start(f32[32,1,8]{2,1,0:T(1,128)} %bitcast.9), calls=%async_computation | async-start | bytes 32768 | tf_op jit(solution)/shard_map/all_to_all | solution.py:59
  137.6 0.6 fusion.21
  138.2 6.5 %all-to-all-done = f32[32,1,8]{2,1,0:T(1,128)S(1)} async-done(((f32[32,1,8]{2,1,0:T(1,128)}), f32[32,1,8]{2,1,0:T(1,128)S(1)}, u32[]{:S(2)}, u32[]{:S(2)}) %all-to-all-start) | async-done | bytes 1056 | tf_op jit(solution)/shard_map/all_to_all | solution.py:59
  144.7 0.6 bitcast_reduce_fusion
  (6 shorter events, 0.0 us)
Async XLA Ops:
  7.2 103.5 %copy-start = (bf16[1,2048]{1,0:T(2,128)(2,1)S(1)}, bf16[1,2048]{1,0:T(2,128)(2,1)}, u32[]{:S(2)}) copy-start(bf16[1,2048]{1,0:T(2,128)(2,1)} %param.11) | copy-start | bytes 12292
  7.2 72.0 %copy-start.2 = (f32[1,8192]{1,0:T(1,128)S(1)}, f32[1,8192]{1,0:T(1,128)}, u32[]{:S(2)}) copy-start(f32[1,8192]{1,0:T(1,128)} %param.8) | copy-start | bytes 98308
  7.2 68.7 %all-gather.2.cloned.1.call-start = ((), (), s32[]{:S(2)}) async-start(), calls=%async_computation.1 | async-start | bytes 4325376 | tf_op jit(solution)/shard_map/all_gather | solution.py:37
  75.9 3.4 %copy-start.1 = (bf16[256,8192]{1,0:T(8,128)(2,1)S(1)}, bf16[256,8192]{1,0:T(8,128)(2,1)}, u32[]{:S(2)}) copy-start(bf16[256,8192]{1,0:T(8,128)(2,1)} %all-gather.2.cloned.1.call-done) | copy-start | bytes 12582916
  135.0 9.7 %all-to-all-start = ((f32[32,1,8]{2,1,0:T(1,128)}), f32[32,1,8]{2,1,0:T(1,128)S(1)}, u32[]{:S(2)}, u32[]{:S(2)}) async-start(f32[32,1,8]{2,1,0:T(1,128)} %bitcast.9), calls=%async_computation | async-start | bytes 32768 | tf_op jit(solution)/shard_map/all_to_all | solution.py:59
Sparse Core Ops, SparseCore 0:
  11.1 64.7 all-gather.1
where the time goes:
time: 152 us
  waiting for transfers between devices  69.6 us (46%)
  matrix products  32.3 us (21%)
  blocking collectives  19.9 us (13%)
  between operations  14.8 us (10%)
  local copies, waits for them, and re-layouts  7.54 us (5%)
  other arithmetic  5.36 us (4%)
  starting transfers between devices  2.6 us (2%)
    all_gather x1, waiting for transfers between devices, body(): lax.all_gather(hidden, ('section', 'shard'), axis=0, tiled=True)  62.5 us
    unnamed x1, blocking collectives  19.9 us
    dot_general x1, matrix products, score_block(): up_out = jnp.dot(normed, up_cols, preferred_element_type=jnp.float32)  15.7 us
    dot_general x1, matrix products, score_block(): gate_out = jnp.dot(normed, gate_cols, preferred_element_type=jnp.float32)  15.6 us
    all_to_all x1, waiting for transfers between devices, body(): lax.all_to_all(spread, ('section', 'shard'), split_axis=0, concat_axis=0,...  6.5 us
    reduce_sum x1, other arithmetic, normalize(): jnp.mean(widened * widened, axis=1, keepdims=True) + epsilon  3.25 us
  transfers between devices with their start and end apart: 2, of which 2 were waited for; matrix products, arithmetic and copies ran while one was open for 4% of the time, Pallas kernels for 0%

commit v1 on v0

v1 whole, which is shorter than its diff:
```python
import functools

import jax
import jax.numpy as jnp
from jax import lax
from jax.experimental import pallas as pl
from jax.experimental.pallas import tpu as pltpu
from jax.sharding import PartitionSpec as P

epsilon = 1e-06
MESH = pl.DeviceIdType.MESH
CHUNKS = 16
COLUMN_TILE = 512
ROW_TILE = 256
LANES = 128
VMEM_BUDGET = 58 * 2**20


def kernel(
    sections, shards, slots,
    hidden_ref, gain_ref, head_ref, pack_ref, owner_ref, gate_ref, up_ref,
    scores_ref, joined_ref,
    rows_buf, inv_buf, gate_ring, up_ring, normed, gate_acc, up_acc, part,
    pack_col, owner_col, message, partials, join_out, join_in,
    ring_sem, line_send, line_recv, z_send, z_recv, sum_send, sum_recv, join_send, join_recv,
):
    chunks, _, depth_z, _, _, half = rows_buf.shape
    width = 2 * half
    total_rows = pack_ref.shape[1]
    own_units = head_ref.shape[1]
    section_rows = total_rows // sections

    section = lax.axis_index("section")
    shard = lax.axis_index("shard")
    x, core = section // 2, section % 2
    z, y = shard // 2, shard % 2
    across_x = (section + 2) % sections
    across_core = 2 * x + 1 - core
    across_y = 1 - y
    shard_y = 2 * z + across_y

    def weight_copies(q):
        slot = q % slots
        rows = pl.ds(pl.multiple_of(q * width, width), width)
        return (
            pltpu.make_async_copy(gate_ref.at[0, rows, :], gate_ring.at[slot], ring_sem.at[slot, 0]),
            pltpu.make_async_copy(up_ref.at[0, rows, :], up_ring.at[slot], ring_sem.at[slot, 1]),
        )

    def load_weights(q):
        for copy in weight_copies(q):
            copy.start()

    pl.loop(0, slots)(load_weights)

    barrier = pltpu.get_barrier_semaphore()
    for step in range(1, shards):
        pl.semaphore_signal(barrier, inc=1, device_id=(section, (shard + step) % shards), device_id_type=MESH)
    for step in range(1, sections):
        pl.semaphore_signal(barrier, inc=1, device_id=((section + step) % sections, shard), device_id_type=MESH)

    widened = hidden_ref[...].astype(jnp.float32)
    inv = lax.rsqrt(jnp.mean(widened * widened, axis=1, keepdims=True) + epsilon)
    inv_buf[section, z, y] = jnp.broadcast_to(inv, inv_buf.shape[3:])
    for q in range(chunks):
        low = widened[:, q * width : q * width + half]
        high = widened[:, q * width + half : (q + 1) * width]
        rows_buf[q, section, z, y] = jnp.concatenate([low, high], axis=0).astype(jnp.bfloat16)

    pl.semaphore_wait(barrier, shards - 1 + sections - 1)

    def line(q, sec, row):
        return inv_buf.at[sec, :, row] if q is None else rows_buf.at[q, sec, :, row]

    def sem_row(q):
        return chunks if q is None else q

    def z_copy(q, step):
        block = inv_buf.at[section, z, y] if q is None else rows_buf.at[q, section, z, y]
        at = sem_row(q)
        return pltpu.make_async_remote_copy(
            src_ref=block, dst_ref=block,
            send_sem=z_send.at[at, step], recv_sem=z_recv.at[at, step],
            device_id=(section, 2 * ((z + step) % depth_z) + y), device_id_type=MESH,
        )

    def line_copy(q, kind):
        if kind == 0:
            source, target = (section, y), (across_x, shard)
        elif kind == 1:
            source, target = (section, y), (section, shard_y)
        elif kind == 2:
            odd = 0 if q is None else q % 2
            source = (across_x + odd * (section - across_x), y + odd * (across_y - y))
            target = (section + odd * (across_x - section), shard_y + odd * (shard - shard_y))
        else:
            source = ((section, y), (across_x, y), (section, across_y), (across_x, across_y))[kind - 3]
            target = (across_core, shard)
        part_line = line(q, *source)
        at = sem_row(q)
        return pltpu.make_async_remote_copy(
            src_ref=part_line, dst_ref=part_line,
            send_sem=line_send.at[at, kind], recv_sem=line_recv.at[at, kind],
            device_id=target, device_id_type=MESH,
        )

    def send_z(q):
        for step in range(1, depth_z):
            z_copy(q, step).start()

    def send_line(q):
        for step in range(1, depth_z):
            z_copy(q, step).wait_recv()
        for kind in (0, 1, 3):
            line_copy(q, kind).start()

    def forward_line(q):
        line_copy(q, 0).wait_recv()
        line_copy(q, 1).wait_recv()
        for kind in (2, 4, 5):
            line_copy(q, kind).start()

    def forward_diagonal(q):
        line_copy(q, 2).wait_recv()
        line_copy(q, 6).start()

    def collect(q):
        for kind in (3, 4, 5, 6):
            line_copy(q, kind).wait_recv()

    send_z(None)
    pl.loop(0, chunks)(send_z)

    sub = lax.broadcasted_iota(jnp.int32, (total_rows, total_rows), 0)
    lane = lax.broadcasted_iota(jnp.int32, (total_rows, total_rows), 1)
    pack_row = pack_ref[pl.ds(section, 1), :]
    pack_col[...] = jnp.sum(jnp.where(sub == lane, pack_row, 0), axis=1, keepdims=True)
    owner_col[...] = jnp.sum(jnp.where(sub == lane, owner_ref[...], 0), axis=1, keepdims=True)

    row_tiles = total_rows // ROW_TILE
    column_tiles = own_units // COLUMN_TILE

    def tile(index):
        rows = pl.ds(pl.multiple_of((index // column_tiles) * ROW_TILE, ROW_TILE), ROW_TILE)
        columns = pl.ds(pl.multiple_of((index % column_tiles) * COLUMN_TILE, COLUMN_TILE), COLUMN_TILE)
        return rows, columns

    @pl.loop(0, row_tiles * column_tiles)
    def _(index):
        at = tile(index)
        gate_acc[at] = jnp.zeros((ROW_TILE, COLUMN_TILE), jnp.float32)
        up_acc[at] = jnp.zeros((ROW_TILE, COLUMN_TILE), jnp.float32)

    part[...] = jnp.zeros_like(part)

    def compute(q):
        for sec in range(sections):
            rows = slice(sec * section_rows, (sec + 1) * section_rows)
            inv_rows = inv_buf[sec].reshape(section_rows, LANES)[:, :1]
            stacked = rows_buf[q, sec].astype(jnp.float32)
            for side in range(2):
                columns = pl.ds(pl.multiple_of(q * width + side * half, half), half)
                values = stacked[:, :, side * 8 : side * 8 + 8, :].reshape(section_rows, half)
                scaled = values * inv_rows * gain_ref[:, columns]
                normed[rows, side * half : (side + 1) * half] = scaled.astype(jnp.bfloat16)
        for copy in weight_copies(q):
            copy.wait()
        slot = q % slots

        @pl.loop(0, row_tiles * column_tiles)
        def _(index):
            rows, columns = tile(index)
            left = normed[rows, :]
            gate_acc[rows, columns] += jnp.dot(left, gate_ring[slot, :, columns], preferred_element_type=jnp.float32)
            up_acc[rows, columns] += jnp.dot(left, up_ring[slot, :, columns], preferred_element_type=jnp.float32)

        @pl.when(q + slots < chunks)
        def _():
            load_weights(q + slots)

    @pl.loop(0, chunks + 3)
    def _(t):
        @pl.when(t == 0)
        def _():
            send_line(None)

        @pl.when(t < chunks)
        def _():
            send_line(t)

        @pl.when(t == 1)
        def _():
            forward_line(None)

        @pl.when(jnp.logical_and(t >= 1, t < chunks + 1))
        def _():
            forward_line(t - 1)

        @pl.when(t == 2)
        def _():
            forward_diagonal(None)

        @pl.when(jnp.logical_and(t >= 2, t < chunks + 2))
        def _():
            forward_diagonal(t - 2)

        @pl.when(t == 3)
        def _():
            collect(None)

        @pl.when(t >= 3)
        def _():
            collect(t - 3)
            compute(t - 3)

    @pl.loop(0, row_tiles * (own_units // LANES))
    def _(index):
        per_row = own_units // LANES
        rows = pl.ds(pl.multiple_of((index // per_row) * ROW_TILE, ROW_TILE), ROW_TILE)
        columns = pl.ds(pl.multiple_of((index % per_row) * LANES, LANES), LANES)
        gate = gate_acc[rows, columns]
        activated = gate / (1.0 + jnp.exp(-gate)) * up_acc[rows, columns]
        part[rows, :] += activated * head_ref[:, columns].astype(jnp.float32)

    own_col = jnp.sum(part[...], axis=1, keepdims=True)
    own_row = jnp.sum(jnp.where(sub == lane, own_col, 0.0), axis=0, keepdims=True)
    message[...] = jnp.broadcast_to(own_row, message.shape)
    partials[shard] = message[...]

    def sum_copy(step):
        return pltpu.make_async_remote_copy(
            src_ref=message, dst_ref=partials.at[shard],
            send_sem=sum_send.at[step], recv_sem=sum_recv.at[step],
            device_id=(section, (shard + step) % shards), device_id_type=MESH,
        )

    for step in range(1, shards):
        sum_copy(step).start()

    def finish_sends(q):
        for step in range(1, depth_z):
            z_copy(q, step).wait_send()
        for kind in range(7):
            line_copy(q, kind).wait_send()

    finish_sends(None)
    pl.loop(0, chunks)(finish_sends)

    for step in range(1, shards):
        sum_copy(step).wait_recv()
    scores = partials[0]
    for other in range(1, shards):
        scores = scores + partials[other]
    scores = scores[:1, :]
    flipped = section % 2 == 1
    log_sigmoid = jnp.minimum(scores, 0.0) - jnp.log1p(jnp.exp(-jnp.abs(scores)))
    values = jnp.where(flipped, log_sigmoid, scores)
    value_col = jnp.sum(jnp.where(sub == lane, values, 0.0), axis=1, keepdims=True)

    lanes = lax.broadcasted_iota(jnp.int32, (total_rows, LANES), 1)
    own_count = joined_ref.shape[1]
    pack_rows = scores_ref.shape[1]

    def owned_by(sec):
        base = (sec * shards + shard) * own_count
        return jnp.sum(jnp.where(owner_col[...] == base + lanes, value_col, 0.0), axis=0, keepdims=True)

    def join_copy(step):
        return pltpu.make_async_remote_copy(
            src_ref=join_out.at[step], dst_ref=join_in.at[section],
            send_sem=join_send.at[step], recv_sem=join_recv.at[step],
            device_id=((section + step) % sections, shard), device_id_type=MESH,
        )

    for step in range(1, sections):
        join_out[step] = jnp.broadcast_to(owned_by((section + step) % sections), join_out.shape[1:])
        join_copy(step).start()
    join_in[section] = jnp.broadcast_to(owned_by(section), join_in.shape[1:])

    base = shard * pack_rows
    packed = jnp.sum(jnp.where(pack_col[...] == base + lanes, value_col, 0.0), axis=0, keepdims=True)
    scores_ref[...] = packed[:, :pack_rows]

    for step in range(1, sections):
        join_copy(step).wait_recv()
    for sec in range(sections):
        joined_ref[sec : sec + 1, :] = join_in[sec][:1, :own_count]

    for step in range(1, shards):
        sum_copy(step).wait_send()
    for step in range(1, sections):
        join_copy(step).wait_send()


def body(sections, shards, hidden, norm_gain, gate_weight, up_weight, head_vector, pack_slot, owner_slot):
    total_rows = owner_slot.shape[0]
    width = hidden.shape[1]
    own_units = head_vector.shape[1]
    half = width // CHUNKS // 2
    depth_z = shards // 2
    line_kinds = 7
    fixed = total_rows * (width * 2 + own_units * 8 + 2 * half * 2 + LANES * 4 * 4)
    fixed += shards * total_rows * 32 + 4 * 2**20
    slot_bytes = 2 * (width // CHUNKS) * own_units * 2
    slots = max(1, min(CHUNKS, (VMEM_BUDGET - fixed) // slot_bytes))
    vmem, dma = pltpu.VMEM, pltpu.SemaphoreType.DMA
    flops = 4 * total_rows * width * own_units
    return pl.pallas_call(
        functools.partial(kernel, sections, shards, slots),
        out_shape=(
            jax.ShapeDtypeStruct((1, total_rows // shards), jnp.float32),
            jax.ShapeDtypeStruct((sections, total_rows // (shards * sections)), jnp.float32),
        ),
        in_specs=[pl.BlockSpec(memory_space=vmem)] * 5 + [pl.BlockSpec(memory_space=pl.ANY)] * 2,
        out_specs=(pl.BlockSpec(memory_space=vmem), pl.BlockSpec(memory_space=vmem)),
        scratch_shapes=[
            vmem((CHUNKS, sections, depth_z, 2, 16, half), jnp.bfloat16),
            vmem((sections, depth_z, 2, 8, LANES), jnp.float32),
            vmem((slots, 2 * half, own_units), jnp.bfloat16),
            vmem((slots, 2 * half, own_units), jnp.bfloat16),
            vmem((total_rows, 2 * half), jnp.bfloat16),
            vmem((total_rows, own_units), jnp.float32),
            vmem((total_rows, own_units), jnp.float32),
            vmem((total_rows, LANES), jnp.float32),
            vmem((total_rows, 1), jnp.int32),
            vmem((total_rows, 1), jnp.int32),
            vmem((8, total_rows), jnp.float32),
            vmem((shards, 8, total_rows), jnp.float32),
            vmem((sections, 8, LANES), jnp.float32),
            vmem((sections, 8, LANES), jnp.float32),
            dma((slots, 2)),
            dma((CHUNKS + 1, line_kinds)),
            dma((CHUNKS + 1, line_kinds)),
            dma((CHUNKS + 1, depth_z)),
            dma((CHUNKS + 1, depth_z)),
            dma((shards,)),
            dma((shards,)),
            dma((sections,)),
            dma((sections,)),
        ],
        compiler_params=pltpu.CompilerParams(
            collective_id=0, has_side_effects=True, vmem_limit_bytes=VMEM_BUDGET + 3 * 2**20
        ),
        cost_estimate=pl.CostEstimate(
            flops=flops, bytes_accessed=4 * width * own_units, transcendentals=total_rows * own_units
        ),
    )(hidden, norm_gain, head_vector, pack_slot, owner_slot[None, :], gate_weight, up_weight)


def solution(mesh):
    in_specs = (
        P(("section", "shard"), None),
        P("section", None),
        P("section", None, "shard"),
        P("section", None, "shard"),
        P("section", "shard"),
        P(),
        P(),
    )
    out_specs = (P("section", "shard"), P(None, ("section", "shard")))
    run = functools.partial(body, mesh.shape["section"], mesh.shape["shard"])
    return jax.shard_map(run, mesh=mesh, in_specs=in_specs, out_specs=out_specs, check_vma=False)
```

time: 152 us -> 75.7 us (0.50)
  Pallas kernels: 0 us -> 72.5 us
  waiting for transfers between devices: 69.6 us -> 0 us
  matrix products: 32.3 us -> 0 us
  blocking collectives: 19.9 us -> 0 us
  between operations: 14.8 us -> 0.64 us
  other arithmetic: 5.36 us -> 0 us
  local copies, waits for them, and re-layouts: 7.54 us -> 2.39 us
  starting transfers between devices: 2.6 us -> 0 us
    pallas_call x0 -> x1, Pallas kernels: none -> 72.5 us  [body(): pl.pallas_call(functools.partial(kernel, sections, shards, slots), out_sh...]
    all_gather x1 -> x0, waiting for transfers between devices: 62.5 us -> none  [body(): lax.all_gather(hidden, ('section', 'shard'), axis=0, tiled=True)]
    dot_general x3 -> x0, matrix products: 32.3 us -> none  [the longest x1 15.7 us: score_block(): up_out = jnp.dot(normed, up_cols, preferred_element_type=jnp.float32)]
    unnamed x1 -> x0, blocking collectives: 19.9 us -> none
    all_to_all x1 -> x0, waiting for transfers between devices: 6.5 us -> none  [body(): lax.all_to_all(spread, ('section', 'shard'), split_axis=0, concat_axis=0,...]
    reduce_sum x2 -> x0, other arithmetic: 3.85 us -> none  [the longest x1 3.25 us: normalize(): jnp.mean(widened * widened, axis=1, keepdims=True) + epsilon]
    gather x2 -> x0, local copies, waits for them, and re-layouts: 3.35 us -> none  [the longest x1 1.96 us: body(): packed = partial_value[inverse]]
    all_to_all x1 -> x0, starting transfers between devices: 2.57 us -> none  [body(): lax.all_to_all(spread, ('section', 'shard'), split_axis=0, concat_axis=0,...]
  transfers between devices with their start and end apart: 2 -> 0, of which waited for: 2 -> 0; matrix products, arithmetic and copies ran while one was open for 4% -> 0% of each run, Pallas kernels for 0% -> 0%
where the time goes in v1:
time: 75.7 us; the launch traced here: 75.6 us
  Pallas kernels  72.5 us (96%)
  local copies, waits for them, and re-layouts  2.39 us (3%)
    pallas_call x1, Pallas kernels, body(): pl.pallas_call(functools.partial(kernel, sections, shards, slots), out_sh...  72.5 us
    unnamed x2, local copies, waits for them, and re-layouts  2.39 us

profile of v1, /device:TPU:0, one launch (start us, length us, event | category | flops | bytes accessed | tf_op | source)
XLA Modules:
  0.0 75.6 jit_solution(13940248512908095632)
XLA Ops:
  0.6 72.5 %shard_map.86 = (f32[1,32]{1,0:T(1,128)}, f32[4,8]{1,0:T(4,128)}) custom-call(bf16[8,8192]{1,0:T(8,128)(2,1)} %hidden_ref.1, f32[1,8192]{1,0:T(1,128)} %gain_ref.1, bf16[1,2048]{1,0:T(2,128)(2,1)} %head_ref.1, s32[4,256]{1,0:T(4,128)} %pack_ref.1, s32[1,256]{1,0:T(1,128)} %bitcast.1, bf16[1,8192,2048]{2,1,0:T(8,128)(2,1)} %gate_ref.1, ...), custom_call_target="tpu_custom_call" | custom-call | flops 17179869184 | bytes 67108864 | tf_op jit(solution)/shard_map/pallas_call | solution.py:308
  73.2 1.1 %copy.11 = f32[1,32]{1,0:T(1,128)} copy(f32[1,32]{1,0:T(1,128)} %get-tuple-element.4) | data formatting | bytes 256
  74.3 1.2 %copy.12 = f32[4,8]{1,0:T(4,128)} copy(f32[4,8]{1,0:T(4,128)} %get-tuple-element.5) | data formatting | bytes 256

commit v2 on v1

--- a/solution.py
+++ b/solution.py
@@ -9,8 +9,10 @@
 
 epsilon = 1e-06
 MESH = pl.DeviceIdType.MESH
-CHUNKS = 16
-COLUMN_TILE = 512
+CHUNKS = 8
+COLUMN_TILE = 1024
+UNIT_TILE = 256
+EARLY_SLOTS = 2
 ROW_TILE = 256
 LANES = 128
 VMEM_BUDGET = 58 * 2**20
@@ -19,7 +21,7 @@
 def kernel(
     sections, shards, slots,
     hidden_ref, gain_ref, head_ref, pack_ref, owner_ref, gate_ref, up_ref,
-    scores_ref, joined_ref,
+    result_ref,
     rows_buf, inv_buf, gate_ring, up_ring, normed, gate_acc, up_acc, part,
     pack_col, owner_col, message, partials, join_out, join_in,
     ring_sem, line_send, line_recv, z_send, z_recv, sum_send, sum_recv, join_send, join_recv,
@@ -51,7 +53,7 @@
         for copy in weight_copies(q):
             copy.start()
 
-    pl.loop(0, slots)(load_weights)
+    pl.loop(0, min(EARLY_SLOTS, slots))(load_weights)
 
     barrier = pltpu.get_barrier_semaphore()
     for step in range(1, shards):
@@ -130,6 +132,7 @@
 
     send_z(None)
     pl.loop(0, chunks)(send_z)
+    pl.loop(min(EARLY_SLOTS, slots), slots)(load_weights)
 
     sub = lax.broadcasted_iota(jnp.int32, (total_rows, total_rows), 0)
     lane = lax.broadcasted_iota(jnp.int32, (total_rows, total_rows), 1)
@@ -156,23 +159,30 @@
     def compute(q):
         for sec in range(sections):
             rows = slice(sec * section_rows, (sec + 1) * section_rows)
-            inv_rows = inv_buf[sec].reshape(section_rows, LANES)[:, :1]
-            stacked = rows_buf[q, sec].astype(jnp.float32)
-            for side in range(2):
-                columns = pl.ds(pl.multiple_of(q * width + side * half, half), half)
-                values = stacked[:, :, side * 8 : side * 8 + 8, :].reshape(section_rows, half)
-                scaled = values * inv_rows * gain_ref[:, columns]
-                normed[rows, side * half : (side + 1) * half] = scaled.astype(jnp.bfloat16)
+            inv_rows = inv_buf[sec].reshape(section_rows, LANES)
+            for start in range(0, half, LANES):
+                stacked = rows_buf[q, sec, :, :, :, start : start + LANES].astype(jnp.float32)
+                for side in range(2):
+                    at = side * half + start
+                    columns = pl.ds(pl.multiple_of(q * width + at, LANES), LANES)
+                    values = stacked[:, :, side * 8 : side * 8 + 8, :].reshape(section_rows, LANES)
+                    scaled = values * inv_rows * gain_ref[:, columns]
+                    normed[rows, at : at + LANES] = scaled.astype(jnp.bfloat16)
         for copy in weight_copies(q):
             copy.wait()
         slot = q % slots
 
         @pl.loop(0, row_tiles * column_tiles)
         def _(index):
-            rows, columns = tile(index)
+            rows, _ = tile(index)
             left = normed[rows, :]
-            gate_acc[rows, columns] += jnp.dot(left, gate_ring[slot, :, columns], preferred_element_type=jnp.float32)
-            up_acc[rows, columns] += jnp.dot(left, up_ring[slot, :, columns], preferred_element_type=jnp.float32)
+            first = (index % column_tiles) * COLUMN_TILE
+            for start in range(0, COLUMN_TILE, UNIT_TILE):
+                columns = pl.ds(pl.multiple_of(first + start, UNIT_TILE), UNIT_TILE)
+                for ring, total in ((gate_ring, gate_acc), (up_ring, up_acc)):
+                    total[rows, columns] += jnp.dot(
+                        left, ring[slot, :, columns], preferred_element_type=jnp.float32
+                    )
 
         @pl.when(q + slots < chunks)
         def _():
@@ -258,8 +268,8 @@
     value_col = jnp.sum(jnp.where(sub == lane, values, 0.0), axis=1, keepdims=True)
 
     lanes = lax.broadcasted_iota(jnp.int32, (total_rows, LANES), 1)
-    own_count = joined_ref.shape[1]
-    pack_rows = scores_ref.shape[1]
+    own_count = total_rows // (sections * shards)
+    pack_rows = total_rows // shards
 
     def owned_by(sec):
         base = (sec * shards + shard) * own_count
@@ -279,12 +289,12 @@
 
     base = shard * pack_rows
     packed = jnp.sum(jnp.where(pack_col[...] == base + lanes, value_col, 0.0), axis=0, keepdims=True)
-    scores_ref[...] = packed[:, :pack_rows]
+    result_ref[sections:, :] = jnp.broadcast_to(packed, (result_ref.shape[0] - sections, LANES))
 
     for step in range(1, sections):
         join_copy(step).wait_recv()
     for sec in range(sections):
-        joined_ref[sec : sec + 1, :] = join_in[sec][:1, :own_count]
+        result_ref[sec : sec + 1, :] = join_in[sec][:1, :]
 
     for step in range(1, shards):
         sum_copy(step).wait_send()
@@ -305,14 +315,11 @@
     slots = max(1, min(CHUNKS, (VMEM_BUDGET - fixed) // slot_bytes))
     vmem, dma = pltpu.VMEM, pltpu.SemaphoreType.DMA
     flops = 4 * total_rows * width * own_units
-    return pl.pallas_call(
+    result = pl.pallas_call(
         functools.partial(kernel, sections, shards, slots),
-        out_shape=(
-            jax.ShapeDtypeStruct((1, total_rows // shards), jnp.float32),
-            jax.ShapeDtypeStruct((sections, total_rows // (shards * sections)), jnp.float32),
-        ),
+        out_shape=jax.ShapeDtypeStruct((2 * sections, LANES), jnp.float32),
         in_specs=[pl.BlockSpec(memory_space=vmem)] * 5 + [pl.BlockSpec(memory_space=pl.ANY)] * 2,
-        out_specs=(pl.BlockSpec(memory_space=vmem), pl.BlockSpec(memory_space=vmem)),
+        out_specs=pl.BlockSpec(memory_space=vmem),
         scratch_shapes=[
             vmem((CHUNKS, sections, depth_z, 2, 16, half), jnp.bfloat16),
             vmem((sections, depth_z, 2, 8, LANES), jnp.float32),
@@ -345,6 +352,10 @@
             flops=flops, bytes_accessed=4 * width * own_units, transcendentals=total_rows * own_units
         ),
     )(hidden, norm_gain, head_vector, pack_slot, owner_slot[None, :], gate_weight, up_weight)
+    return (
+        result[sections : sections + 1, : total_rows // shards],
+        result[:sections, : total_rows // (sections * shards)],
+    )
 
 
 def solution(mesh):

time: 75.7 us -> 62 us (0.82)
  Pallas kernels: 72.5 us -> 58.7 us
    pallas_call x1, Pallas kernels: 72.5 us -> 58.7 us  [body(): pl.pallas_call(functools.partial(kernel, sections, shards, slots), out_sh...]
    slice x0 -> x2, local copies, waits for them, and re-layouts: none -> 2.45 us  [the longest x1 1.26 us: body(): result[:sections, :total_rows // (sections * shards)]]
    unnamed x2 -> x0, local copies, waits for them, and re-layouts: 2.39 us -> none
where the time goes in v2:
time: 62 us; the launch traced here: 61.8 us
  Pallas kernels  58.7 us (95%)
  local copies, waits for them, and re-layouts  2.45 us (4%)
  between operations  0.64 us (1%)
    pallas_call x1, Pallas kernels, body(): pl.pallas_call(functools.partial(kernel, sections, shards, slots), out_sh...  58.7 us
    slice x1, local copies, waits for them, and re-layouts, body(): result[:sections, :total_rows // (sections * shards)]  1.26 us

profile of v2, /device:TPU:0, one launch (start us, length us, event | category | flops | bytes accessed | tf_op | source)
XLA Modules:
  0.0 61.8 jit_solution(15383004084260847415)
XLA Ops:
  0.6 58.7 %shard_map.86 = f32[8,128]{1,0:T(8,128)} custom-call(bf16[8,8192]{1,0:T(8,128)(2,1)} %hidden_ref.1, f32[1,8192]{1,0:T(1,128)} %gain_ref.1, bf16[1,2048]{1,0:T(2,128)(2,1)} %head_ref.1, s32[4,256]{1,0:T(4,128)} %pack_ref.1, s32[1,256]{1,0:T(1,128)} %bitcast.1, bf16[1,8192,2048]{2,1,0:T(8,128)(2,1)} %gate_ref.1, bf16[1,8192,2048]{2,1,0:T(8,128)(2,1)} %up_ref.1), custom_call_target="tpu_custom_call" | custom-call | flops 17179869184 | bytes 67108864 | tf_op jit(solution)/shard_map/pallas_call | solution.py:318
  59.3 1.2 %slice.6 = f32[1,32]{1,0:T(1,128)} slice(f32[8,128]{1,0:T(8,128)} %shard_map.86), slice={[4:5], [0:32]} | slice | bytes 256 | tf_op jit(solution)/shard_map/slice | solution.py:356
  60.5 1.3 %slice.7 = f32[4,8]{1,0:T(4,128)} slice(f32[8,128]{1,0:T(8,128)} %shard_map.86), slice={[0:4], [0:8]} | slice | bytes 256 | tf_op jit(solution)/shard_map/slice | solution.py:357

commit v3 on v2

--- a/solution.py
+++ b/solution.py
@@ -9,8 +9,8 @@
 
 epsilon = 1e-06
 MESH = pl.DeviceIdType.MESH
-CHUNKS = 8
-COLUMN_TILE = 1024
+CHUNKS = 16
+GROUP = 2
 UNIT_TILE = 256
 EARLY_SLOTS = 2
 ROW_TILE = 256
@@ -28,6 +28,7 @@
 ):
     chunks, _, depth_z, _, _, half = rows_buf.shape
     width = 2 * half
+    depth = GROUP * width
     total_rows = pack_ref.shape[1]
     own_units = head_ref.shape[1]
     section_rows = total_rows // sections
@@ -43,7 +44,7 @@
 
     def weight_copies(q):
         slot = q % slots
-        rows = pl.ds(pl.multiple_of(q * width, width), width)
+        rows = pl.ds(pl.multiple_of(q * depth, depth), depth)
         return (
             pltpu.make_async_copy(gate_ref.at[0, rows, :], gate_ring.at[slot], ring_sem.at[slot, 0]),
             pltpu.make_async_copy(up_ref.at[0, rows, :], up_ring.at[slot], ring_sem.at[slot, 1]),
@@ -141,22 +142,19 @@
     owner_col[...] = jnp.sum(jnp.where(sub == lane, owner_ref[...], 0), axis=1, keepdims=True)
 
     row_tiles = total_rows // ROW_TILE
-    column_tiles = own_units // COLUMN_TILE
-
-    def tile(index):
-        rows = pl.ds(pl.multiple_of((index // column_tiles) * ROW_TILE, ROW_TILE), ROW_TILE)
-        columns = pl.ds(pl.multiple_of((index % column_tiles) * COLUMN_TILE, COLUMN_TILE), COLUMN_TILE)
-        return rows, columns
-
-    @pl.loop(0, row_tiles * column_tiles)
+
+    @pl.loop(0, total_rows // ROW_TILE)
     def _(index):
-        at = tile(index)
-        gate_acc[at] = jnp.zeros((ROW_TILE, COLUMN_TILE), jnp.float32)
-        up_acc[at] = jnp.zeros((ROW_TILE, COLUMN_TILE), jnp.float32)
+        rows = pl.ds(pl.multiple_of(index * ROW_TILE, ROW_TILE), ROW_TILE)
+        gate_acc[rows, :] = jnp.zeros((ROW_TILE, own_units), jnp.float32)
+        up_acc[rows, :] = jnp.zeros((ROW_TILE, own_units), jnp.float32)
 
     part[...] = jnp.zeros_like(part)
 
-    def compute(q):
+    steps = chunks // GROUP
+    half_units = own_units // 2
+
+    def normalise(q, place):
         for sec in range(sections):
             rows = slice(sec * section_rows, (sec + 1) * section_rows)
             inv_rows = inv_buf[sec].reshape(section_rows, LANES)
@@ -167,61 +165,74 @@
                     columns = pl.ds(pl.multiple_of(q * width + at, LANES), LANES)
                     values = stacked[:, :, side * 8 : side * 8 + 8, :].reshape(section_rows, LANES)
                     scaled = values * inv_rows * gain_ref[:, columns]
-                    normed[rows, at : at + LANES] = scaled.astype(jnp.bfloat16)
-        for copy in weight_copies(q):
+                    normed[rows, place * width + at : place * width + at + LANES] = scaled.astype(jnp.bfloat16)
+
+    def prepare(step):
+        for place in range(GROUP):
+            normalise(step * GROUP + place, place)
+        for copy in weight_copies(step):
             copy.wait()
-        slot = q % slots
-
-        @pl.loop(0, row_tiles * column_tiles)
-        def _(index):
-            rows, _ = tile(index)
+
+    def multiply(step, side):
+        slot = step % slots
+
+        def row_tile(index):
+            rows = pl.ds(pl.multiple_of(index * ROW_TILE, ROW_TILE), ROW_TILE)
             left = normed[rows, :]
-            first = (index % column_tiles) * COLUMN_TILE
-            for start in range(0, COLUMN_TILE, UNIT_TILE):
-                columns = pl.ds(pl.multiple_of(first + start, UNIT_TILE), UNIT_TILE)
+            for start in range(0, half_units, UNIT_TILE):
+                columns = pl.ds(pl.multiple_of(side * half_units + start, UNIT_TILE), UNIT_TILE)
                 for ring, total in ((gate_ring, gate_acc), (up_ring, up_acc)):
                     total[rows, columns] += jnp.dot(
                         left, ring[slot, :, columns], preferred_element_type=jnp.float32
                     )
 
-        @pl.when(q + slots < chunks)
+        pl.loop(0, row_tiles)(row_tile)
+
+    send_line(None)
+    send_line(0)
+    forward_line(None)
+    send_line(1)
+    forward_line(0)
+    forward_diagonal(None)
+    send_line(2)
+    forward_line(1)
+    forward_diagonal(0)
+    send_line(3)
+    forward_line(2)
+    forward_diagonal(1)
+    collect(None)
+    collect(0)
+    send_line(4)
+    forward_line(3)
+    forward_diagonal(2)
+    collect(1)
+
+    @pl.loop(0, 2 * steps)
+    def _(u):
+        def advance(act, q, limit):
+            @pl.when(jnp.logical_and(u > 0, jnp.logical_and(q < limit, q < chunks)))
+            def _():
+                act(q)
+
+        for ahead in range(2):
+            advance(send_line, 3 + 2 * u + ahead, 5 + 2 * u)
+        for ahead in range(2):
+            advance(forward_line, 4 + (3 * (u - 1 + steps * 2)) // 2 - 3 * steps + ahead, 4 + (3 * u) // 2)
+        for ahead in range(2):
+            advance(forward_diagonal, 3 + (5 * (u + 3)) // 4 - 5 + ahead, 3 + (5 * u) // 4)
+        advance(collect, u + 1, u + 2)
+
+        step, side = u // 2, u % 2
+
+        @pl.when(side == 0)
         def _():
-            load_weights(q + slots)
-
-    @pl.loop(0, chunks + 3)
-    def _(t):
-        @pl.when(t == 0)
+            prepare(step)
+
+        multiply(step, side)
+
+        @pl.when(jnp.logical_and(side == 1, step + slots < steps))
         def _():
-            send_line(None)
-
-        @pl.when(t < chunks)
-        def _():
-            send_line(t)
-
-        @pl.when(t == 1)
-        def _():
-            forward_line(None)
-
-        @pl.when(jnp.logical_and(t >= 1, t < chunks + 1))
-        def _():
-            forward_line(t - 1)
-
-        @pl.when(t == 2)
-        def _():
-            forward_diagonal(None)
-
-        @pl.when(jnp.logical_and(t >= 2, t < chunks + 2))
-        def _():
-            forward_diagonal(t - 2)
-
-        @pl.when(t == 3)
-        def _():
-            collect(None)
-
-        @pl.when(t >= 3)
-        def _():
-            collect(t - 3)
-            compute(t - 3)
+            load_weights(step + slots)
 
     @pl.loop(0, row_tiles * (own_units // LANES))
     def _(index):
@@ -311,8 +322,8 @@
     line_kinds = 7
     fixed = total_rows * (width * 2 + own_units * 8 + 2 * half * 2 + LANES * 4 * 4)
     fixed += shards * total_rows * 32 + 4 * 2**20
-    slot_bytes = 2 * (width // CHUNKS) * own_units * 2
-    slots = max(1, min(CHUNKS, (VMEM_BUDGET - fixed) // slot_bytes))
+    slot_bytes = 2 * GROUP * (width // CHUNKS) * own_units * 2
+    slots = max(1, min(CHUNKS // GROUP, (VMEM_BUDGET - fixed) // slot_bytes))
     vmem, dma = pltpu.VMEM, pltpu.SemaphoreType.DMA
     flops = 4 * total_rows * width * own_units
     result = pl.pallas_call(
@@ -323,9 +334,9 @@
         scratch_shapes=[
             vmem((CHUNKS, sections, depth_z, 2, 16, half), jnp.bfloat16),
             vmem((sections, depth_z, 2, 8, LANES), jnp.float32),
-            vmem((slots, 2 * half, own_units), jnp.bfloat16),
-            vmem((slots, 2 * half, own_units), jnp.bfloat16),
-            vmem((total_rows, 2 * half), jnp.bfloat16),
+            vmem((slots, GROUP * 2 * half, own_units), jnp.bfloat16),
+            vmem((slots, GROUP * 2 * half, own_units), jnp.bfloat16),
+            vmem((total_rows, GROUP * 2 * half), jnp.bfloat16),
             vmem((total_rows, own_units), jnp.float32),
             vmem((total_rows, own_units), jnp.float32),
             vmem((total_rows, LANES), jnp.float32),

time: 62 us -> 70.1 us (1.13)
  Pallas kernels: 58.7 us -> 66.8 us
    pallas_call x1, Pallas kernels: 58.7 us -> 66.8 us  [body(): pl.pallas_call(functools.partial(kernel, sections, shards, slots), out_sh...]
where the time goes in v3:
time: 70.1 us; the launch traced here: 69.9 us
  Pallas kernels  66.8 us (95%)
  local copies, waits for them, and re-layouts  2.45 us (3%)
    pallas_call x1, Pallas kernels, body(): pl.pallas_call(functools.partial(kernel, sections, shards, slots), out_sh...  66.8 us

profile of v3, /device:TPU:0, one launch (start us, length us, event | category | flops | bytes accessed | tf_op | source)
XLA Modules:
  0.0 69.9 jit_solution(6001389391631580888)
XLA Ops:
  0.6 66.8 %shard_map.86 = f32[8,128]{1,0:T(8,128)} custom-call(bf16[8,8192]{1,0:T(8,128)(2,1)} %hidden_ref.1, f32[1,8192]{1,0:T(1,128)} %gain_ref.1, bf16[1,2048]{1,0:T(2,128)(2,1)} %head_ref.1, s32[4,256]{1,0:T(4,128)} %pack_ref.1, s32[1,256]{1,0:T(1,128)} %bitcast.1, bf16[1,8192,2048]{2,1,0:T(8,128)(2,1)} %gate_ref.1, bf16[1,8192,2048]{2,1,0:T(8,128)(2,1)} %up_ref.1), custom_call_target="tpu_custom_call" | custom-call | flops 17179869184 | bytes 67108864 | tf_op jit(solution)/shard_map/pallas_call | solution.py:329
  67.4 1.2 %slice.6 = f32[1,32]{1,0:T(1,128)} slice(f32[8,128]{1,0:T(8,128)} %shard_map.86), slice={[4:5], [0:32]} | slice | bytes 256 | tf_op jit(solution)/shard_map/slice | solution.py:367
  68.6 1.3 %slice.7 = f32[4,8]{1,0:T(4,128)} slice(f32[8,128]{1,0:T(8,128)} %shard_map.86), slice={[0:4], [0:8]} | slice | bytes 256 | tf_op jit(solution)/shard_map/slice | solution.py:368

commit v4 on v2

--- a/solution.py
+++ b/solution.py
@@ -11,7 +11,7 @@
 MESH = pl.DeviceIdType.MESH
 CHUNKS = 8
 COLUMN_TILE = 1024
-UNIT_TILE = 256
+UNIT_TILE = 512
 EARLY_SLOTS = 2
 ROW_TILE = 256
 LANES = 128
@@ -26,7 +26,7 @@
     pack_col, owner_col, message, partials, join_out, join_in,
     ring_sem, line_send, line_recv, z_send, z_recv, sum_send, sum_recv, join_send, join_recv,
 ):
-    chunks, _, depth_z, _, _, half = rows_buf.shape
+    chunks, _, _, depth_z, _, half = rows_buf.shape
     width = 2 * half
     total_rows = pack_ref.shape[1]
     own_units = head_ref.shape[1]
@@ -63,22 +63,25 @@
 
     widened = hidden_ref[...].astype(jnp.float32)
     inv = lax.rsqrt(jnp.mean(widened * widened, axis=1, keepdims=True) + epsilon)
-    inv_buf[section, z, y] = jnp.broadcast_to(inv, inv_buf.shape[3:])
+    inv_buf[section, y, z] = jnp.broadcast_to(inv, inv_buf.shape[3:])
     for q in range(chunks):
         low = widened[:, q * width : q * width + half]
         high = widened[:, q * width + half : (q + 1) * width]
-        rows_buf[q, section, z, y] = jnp.concatenate([low, high], axis=0).astype(jnp.bfloat16)
+        rows_buf[q, section, y, z] = jnp.concatenate([low, high], axis=0).astype(jnp.bfloat16)
 
     pl.semaphore_wait(barrier, shards - 1 + sections - 1)
 
     def line(q, sec, row):
-        return inv_buf.at[sec, :, row] if q is None else rows_buf.at[q, sec, :, row]
+        return inv_buf.at[sec, row] if q is None else rows_buf.at[q, sec, row]
+
+    def plane(q, sec):
+        return inv_buf.at[sec] if q is None else rows_buf.at[q, sec]
 
     def sem_row(q):
         return chunks if q is None else q
 
     def z_copy(q, step):
-        block = inv_buf.at[section, z, y] if q is None else rows_buf.at[q, section, z, y]
+        block = inv_buf.at[section, y, z] if q is None else rows_buf.at[q, section, y, z]
         at = sem_row(q)
         return pltpu.make_async_remote_copy(
             src_ref=block, dst_ref=block,
@@ -88,20 +91,19 @@
 
     def line_copy(q, kind):
         if kind == 0:
-            source, target = (section, y), (across_x, shard)
+            source, target = line(q, section, y), (across_x, shard)
         elif kind == 1:
-            source, target = (section, y), (section, shard_y)
+            source, target = line(q, section, y), (section, shard_y)
         elif kind == 2:
             odd = 0 if q is None else q % 2
-            source = (across_x + odd * (section - across_x), y + odd * (across_y - y))
+            source = line(q, across_x + odd * (section - across_x), y + odd * (across_y - y))
             target = (section + odd * (across_x - section), shard_y + odd * (shard - shard_y))
         else:
-            source = ((section, y), (across_x, y), (section, across_y), (across_x, across_y))[kind - 3]
+            source = plane(q, section if kind == 3 else across_x)
             target = (across_core, shard)
-        part_line = line(q, *source)
         at = sem_row(q)
         return pltpu.make_async_remote_copy(
-            src_ref=part_line, dst_ref=part_line,
+            src_ref=source, dst_ref=source,
             send_sem=line_send.at[at, kind], recv_sem=line_recv.at[at, kind],
             device_id=target, device_id_type=MESH,
         )
@@ -113,21 +115,21 @@
     def send_line(q):
         for step in range(1, depth_z):
             z_copy(q, step).wait_recv()
-        for kind in (0, 1, 3):
+        for kind in (0, 1):
             line_copy(q, kind).start()
 
     def forward_line(q):
         line_copy(q, 0).wait_recv()
         line_copy(q, 1).wait_recv()
-        for kind in (2, 4, 5):
+        for kind in (2, 3):
             line_copy(q, kind).start()
 
     def forward_diagonal(q):
         line_copy(q, 2).wait_recv()
-        line_copy(q, 6).start()
+        line_copy(q, 4).start()
 
     def collect(q):
-        for kind in (3, 4, 5, 6):
+        for kind in (3, 4):
             line_copy(q, kind).wait_recv()
 
     send_z(None)
@@ -136,9 +138,12 @@
 
     sub = lax.broadcasted_iota(jnp.int32, (total_rows, total_rows), 0)
     lane = lax.broadcasted_iota(jnp.int32, (total_rows, total_rows), 1)
+    in_section = sub % section_rows
+    held_z, held_y = in_section // 8 % depth_z, in_section // (8 * depth_z)
+    token = sub - in_section + (2 * held_z + held_y) * 8 + sub % 8
     pack_row = pack_ref[pl.ds(section, 1), :]
-    pack_col[...] = jnp.sum(jnp.where(sub == lane, pack_row, 0), axis=1, keepdims=True)
-    owner_col[...] = jnp.sum(jnp.where(sub == lane, owner_ref[...], 0), axis=1, keepdims=True)
+    pack_col[...] = jnp.sum(jnp.where(token == lane, pack_row, 0), axis=1, keepdims=True)
+    owner_col[...] = jnp.sum(jnp.where(token == lane, owner_ref[...], 0), axis=1, keepdims=True)
 
     row_tiles = total_rows // ROW_TILE
     column_tiles = own_units // COLUMN_TILE
@@ -250,7 +255,7 @@
     def finish_sends(q):
         for step in range(1, depth_z):
             z_copy(q, step).wait_send()
-        for kind in range(7):
+        for kind in range(5):
             line_copy(q, kind).wait_send()
 
     finish_sends(None)
@@ -302,13 +307,19 @@
         join_copy(step).wait_send()
 
 
+def part_result(result_ref, scores_ref, joined_ref):
+    sections = joined_ref.shape[0]
+    scores_ref[...] = result_ref[sections : sections + 1, : scores_ref.shape[1]]
+    joined_ref[...] = result_ref[:sections, : joined_ref.shape[1]]
+
+
 def body(sections, shards, hidden, norm_gain, gate_weight, up_weight, head_vector, pack_slot, owner_slot):
     total_rows = owner_slot.shape[0]
     width = hidden.shape[1]
     own_units = head_vector.shape[1]
     half = width // CHUNKS // 2
     depth_z = shards // 2
-    line_kinds = 7
+    line_kinds = 5
     fixed = total_rows * (width * 2 + own_units * 8 + 2 * half * 2 + LANES * 4 * 4)
     fixed += shards * total_rows * 32 + 4 * 2**20
     slot_bytes = 2 * (width // CHUNKS) * own_units * 2
@@ -321,8 +332,8 @@
         in_specs=[pl.BlockSpec(memory_space=vmem)] * 5 + [pl.BlockSpec(memory_space=pl.ANY)] * 2,
         out_specs=pl.BlockSpec(memory_space=vmem),
         scratch_shapes=[
-            vmem((CHUNKS, sections, depth_z, 2, 16, half), jnp.bfloat16),
-            vmem((sections, depth_z, 2, 8, LANES), jnp.float32),
+            vmem((CHUNKS, sections, 2, depth_z, 16, half), jnp.bfloat16),
+            vmem((sections, 2, depth_z, 8, LANES), jnp.float32),
             vmem((slots, 2 * half, own_units), jnp.bfloat16),
             vmem((slots, 2 * half, own_units), jnp.bfloat16),
             vmem((total_rows, 2 * half), jnp.bfloat16),
@@ -352,10 +363,15 @@
             flops=flops, bytes_accessed=4 * width * own_units, transcendentals=total_rows * own_units
         ),
     )(hidden, norm_gain, head_vector, pack_slot, owner_slot[None, :], gate_weight, up_weight)
-    return (
-        result[sections : sections + 1, : total_rows // shards],
-        result[:sections, : total_rows // (sections * shards)],
-    )
+    return pl.pallas_call(
+        part_result,
+        out_shape=(
+            jax.ShapeDtypeStruct((1, total_rows // shards), jnp.float32),
+            jax.ShapeDtypeStruct((sections, total_rows // (sections * shards)), jnp.float32),
+        ),
+        in_specs=[pl.BlockSpec(memory_space=vmem)],
+        out_specs=(pl.BlockSpec(memory_space=vmem), pl.BlockSpec(memory_space=vmem)),
+    )(result)
 
 
 def solution(mesh):

time: 62 us -> 59.5 us (0.960)
  local copies, waits for them, and re-layouts: 2.45 us -> 0 us
    slice x2 -> x0, local copies, waits for them, and re-layouts: 2.45 us -> none  [the longest x1 1.26 us: body(): result[:sections, :total_rows // (sections * shards)]]
    pallas_call x1, Pallas kernels: 58.7 us -> 57.4 us  [body(): pl.pallas_call(functools.partial(kernel, sections, shards, slots), out_sh...]
    pallas_call x0 -> x1, Pallas kernels: none -> 1.27 us  [body(): pl.pallas_call(part_result, out_shape=(jax.ShapeDtypeStruct((1, total_row...]
where the time goes in v4:
time: 59.5 us; the launch traced here: 59.3 us
  Pallas kernels  58.7 us (99%)
  between operations  0.64 us (1%)
    pallas_call x1, Pallas kernels, body(): pl.pallas_call(functools.partial(kernel, sections, shards, slots), out_sh...  57.4 us
    pallas_call x1, Pallas kernels, body(): pl.pallas_call(part_result, out_shape=(jax.ShapeDtypeStruct((1, total_row...  1.27 us

profile of v4, /device:TPU:0, one launch (start us, length us, event | category | flops | bytes accessed | tf_op | source)
XLA Modules:
  0.0 59.3 jit_solution(17906051900416489698)
XLA Ops:
  0.6 57.4 %shard_map.86.result_ref = f32[8,128]{1,0:T(8,128)} custom-call(bf16[8,8192]{1,0:T(8,128)(2,1)} %hidden_ref.1, f32[1,8192]{1,0:T(1,128)} %gain_ref.1, bf16[1,2048]{1,0:T(2,128)(2,1)} %head_ref.1, s32[4,256]{1,0:T(4,128)} %pack_ref.1, s32[1,256]{1,0:T(1,128)} %bitcast.1, bf16[1,8192,2048]{2,1,0:T(8,128)(2,1)} %gate_ref.1, bf16[1,8192,2048]{2,1,0:T(8,128)(2,1)} %up_ref.1), custom_call_target="tpu_custom_call" | custom-call | flops 17179869184 | bytes 67108864 | tf_op jit(solution)/shard_map/pallas_call | solution.py:329
  58.0 1.3 %shard_map.87 = (f32[1,32]{1,0:T(1,128)}, f32[4,8]{1,0:T(4,128)}) custom-call(f32[8,128]{1,0:T(8,128)} %shard_map.86.result_ref), custom_call_target="tpu_custom_call" | custom-call | tf_op jit(solution)/shard_map/pallas_call | solution.py:366

commit v5 on v4

--- a/solution.py
+++ b/solution.py
@@ -10,7 +10,6 @@
 epsilon = 1e-06
 MESH = pl.DeviceIdType.MESH
 CHUNKS = 8
-COLUMN_TILE = 1024
 UNIT_TILE = 512
 EARLY_SLOTS = 2
 ROW_TILE = 256
@@ -53,13 +52,13 @@
         for copy in weight_copies(q):
             copy.start()
 
-    pl.loop(0, min(EARLY_SLOTS, slots))(load_weights)
-
     barrier = pltpu.get_barrier_semaphore()
     for step in range(1, shards):
         pl.semaphore_signal(barrier, inc=1, device_id=(section, (shard + step) % shards), device_id_type=MESH)
     for step in range(1, sections):
         pl.semaphore_signal(barrier, inc=1, device_id=((section + step) % sections, shard), device_id_type=MESH)
+
+    pl.loop(0, min(EARLY_SLOTS, slots))(load_weights)
 
     widened = hidden_ref[...].astype(jnp.float32)
     inv = lax.rsqrt(jnp.mean(widened * widened, axis=1, keepdims=True) + epsilon)
@@ -132,36 +131,10 @@
         for kind in (3, 4):
             line_copy(q, kind).wait_recv()
 
-    send_z(None)
-    pl.loop(0, chunks)(send_z)
-    pl.loop(min(EARLY_SLOTS, slots), slots)(load_weights)
-
-    sub = lax.broadcasted_iota(jnp.int32, (total_rows, total_rows), 0)
-    lane = lax.broadcasted_iota(jnp.int32, (total_rows, total_rows), 1)
-    in_section = sub % section_rows
-    held_z, held_y = in_section // 8 % depth_z, in_section // (8 * depth_z)
-    token = sub - in_section + (2 * held_z + held_y) * 8 + sub % 8
-    pack_row = pack_ref[pl.ds(section, 1), :]
-    pack_col[...] = jnp.sum(jnp.where(token == lane, pack_row, 0), axis=1, keepdims=True)
-    owner_col[...] = jnp.sum(jnp.where(token == lane, owner_ref[...], 0), axis=1, keepdims=True)
-
     row_tiles = total_rows // ROW_TILE
-    column_tiles = own_units // COLUMN_TILE
-
-    def tile(index):
-        rows = pl.ds(pl.multiple_of((index // column_tiles) * ROW_TILE, ROW_TILE), ROW_TILE)
-        columns = pl.ds(pl.multiple_of((index % column_tiles) * COLUMN_TILE, COLUMN_TILE), COLUMN_TILE)
-        return rows, columns
-
-    @pl.loop(0, row_tiles * column_tiles)
-    def _(index):
-        at = tile(index)
-        gate_acc[at] = jnp.zeros((ROW_TILE, COLUMN_TILE), jnp.float32)
-        up_acc[at] = jnp.zeros((ROW_TILE, COLUMN_TILE), jnp.float32)
-
-    part[...] = jnp.zeros_like(part)
-
-    def compute(q):
+    half_units = own_units // 2
+
+    def normalise(q):
         for sec in range(sections):
             rows = slice(sec * section_rows, (sec + 1) * section_rows)
             inv_rows = inv_buf[sec].reshape(section_rows, LANES)
@@ -173,60 +146,90 @@
                     values = stacked[:, :, side * 8 : side * 8 + 8, :].reshape(section_rows, LANES)
                     scaled = values * inv_rows * gain_ref[:, columns]
                     normed[rows, at : at + LANES] = scaled.astype(jnp.bfloat16)
-        for copy in weight_copies(q):
-            copy.wait()
+
+    def multiply(q, side):
         slot = q % slots
 
-        @pl.loop(0, row_tiles * column_tiles)
-        def _(index):
-            rows, _ = tile(index)
+        def row_tile(rows):
             left = normed[rows, :]
-            first = (index % column_tiles) * COLUMN_TILE
-            for start in range(0, COLUMN_TILE, UNIT_TILE):
-                columns = pl.ds(pl.multiple_of(first + start, UNIT_TILE), UNIT_TILE)
+            for start in range(side * half_units, (side + 1) * half_units, UNIT_TILE):
+                columns = slice(start, start + UNIT_TILE)
                 for ring, total in ((gate_ring, gate_acc), (up_ring, up_acc)):
                     total[rows, columns] += jnp.dot(
                         left, ring[slot, :, columns], preferred_element_type=jnp.float32
                     )
 
+        if row_tiles == 1:
+            row_tile(slice(0, ROW_TILE))
+        else:
+            pl.loop(0, row_tiles)(
+                lambda index: row_tile(pl.ds(pl.multiple_of(index * ROW_TILE, ROW_TILE), ROW_TILE))
+            )
+
+    send_z(None)
+    for q in range(3):
+        send_z(q)
+
+    @pl.loop(0, row_tiles)
+    def _(index):
+        rows = pl.ds(pl.multiple_of(index * ROW_TILE, ROW_TILE), ROW_TILE)
+        gate_acc[rows, :] = jnp.zeros((ROW_TILE, own_units), jnp.float32)
+        up_acc[rows, :] = jnp.zeros((ROW_TILE, own_units), jnp.float32)
+
+    part[...] = jnp.zeros_like(part)
+
+    send_line(None)
+    send_line(0)
+    pl.loop(3, chunks)(send_z)
+    pl.loop(min(EARLY_SLOTS, slots), slots)(load_weights)
+    forward_line(None)
+    send_line(1)
+    forward_line(0)
+
+    sub = lax.broadcasted_iota(jnp.int32, (total_rows, total_rows), 0)
+    lane = lax.broadcasted_iota(jnp.int32, (total_rows, total_rows), 1)
+    in_section = sub % section_rows
+    held_z, held_y = in_section // 8 % depth_z, in_section // (8 * depth_z)
+    token = sub - in_section + (2 * held_z + held_y) * 8 + sub % 8
+    pack_row = pack_ref[pl.ds(section, 1), :]
+    pack_col[...] = jnp.sum(jnp.where(token == lane, pack_row, 0), axis=1, keepdims=True)
+    owner_col[...] = jnp.sum(jnp.where(token == lane, owner_ref[...], 0), axis=1, keepdims=True)
+
+    forward_diagonal(None)
+    send_line(2)
+    forward_line(1)
+    forward_diagonal(0)
+    collect(None)
+    collect(0)
+
+    @pl.loop(0, chunks)
+    def _(q):
+        for copy in weight_copies(q):
+            copy.wait()
+        normalise(q)
+        multiply(q, 0)
+
+        @pl.when(q + 3 < chunks)
+        def _():
+            send_line(q + 3)
+
+        @pl.when(q + 2 < chunks)
+        def _():
+            forward_line(q + 2)
+
+        @pl.when(q + 1 < chunks)
+        def _():
+            forward_diagonal(q + 1)
+
+        multiply(q, 1)
+
         @pl.when(q + slots < chunks)
         def _():
             load_weights(q + slots)
 
-    @pl.loop(0, chunks + 3)
-    def _(t):
-        @pl.when(t == 0)
-        def _():
-            send_line(None)
-
-        @pl.when(t < chunks)
-        def _():
-            send_line(t)
-
-        @pl.when(t == 1)
-        def _():
-            forward_line(None)
-
-        @pl.when(jnp.logical_and(t >= 1, t < chunks + 1))
-        def _():
-            forward_line(t - 1)
-
-        @pl.when(t == 2)
-        def _():
-            forward_diagonal(None)
-
-        @pl.when(jnp.logical_and(t >= 2, t < chunks + 2))
-        def _():
-            forward_diagonal(t - 2)
-
-        @pl.when(t == 3)
-        def _():
-            collect(None)
-
-        @pl.when(t >= 3)
-        def _():
-            collect(t - 3)
-            compute(t - 3)
+        @pl.when(q + 1 < chunks)
+        def _():
+            collect(q + 1)
 
     @pl.loop(0, row_tiles * (own_units // LANES))
     def _(index):

time: 59.5 us -> 59 us (level)
  no operation moved by 1% of the time
where the time goes in v5:
time: 59 us; the launch traced here: 58.8 us
  Pallas kernels  58.2 us (99%)
  between operations  0.64 us (1%)
    pallas_call x1, Pallas kernels, body(): pl.pallas_call(functools.partial(kernel, sections, shards, slots), out_sh...  56.9 us
    pallas_call x1, Pallas kernels, body(): pl.pallas_call(part_result, out_shape=(jax.ShapeDtypeStruct((1, total_row...  1.27 us

profile of v5, /device:TPU:0, one launch (start us, length us, event | category | flops | bytes accessed | tf_op | source)
XLA Modules:
  0.0 58.8 jit_solution(16480125350333017997)
XLA Ops:
  0.6 56.9 %shard_map.86.result_ref = f32[8,128]{1,0:T(8,128)} custom-call(bf16[8,8192]{1,0:T(8,128)(2,1)} %hidden_ref.1, f32[1,8192]{1,0:T(1,128)} %gain_ref.1, bf16[1,2048]{1,0:T(2,128)(2,1)} %head_ref.1, s32[4,256]{1,0:T(4,128)} %pack_ref.1, s32[1,256]{1,0:T(1,128)} %bitcast.1, bf16[1,8192,2048]{2,1,0:T(8,128)(2,1)} %gate_ref.1, bf16[1,8192,2048]{2,1,0:T(8,128)(2,1)} %up_ref.1), custom_call_target="tpu_custom_call" | custom-call | flops 17179869184 | bytes 67108864 | tf_op jit(solution)/shard_map/pallas_call | solution.py:332
  57.5 1.3 %shard_map.87 = (f32[1,32]{1,0:T(1,128)}, f32[4,8]{1,0:T(4,128)}) custom-call(f32[8,128]{1,0:T(8,128)} %shard_map.86.result_ref), custom_call_target="tpu_custom_call" | custom-call | tf_op jit(solution)/shard_map/pallas_call | solution.py:369
